TPU v7x, 128 devices: a whole 4x4x4 slice. The times are simulated.
128 devices in a mesh: ep: 8 (over z, core), dp: 16 (over y, x).
Axes of the slice: x: 4, y: 4, z: 4, core: 2. Of those that a mesh axis runs over, the one named last changes fastest.
Arguments:
- tokens: bfloat16 [32768, 7168], P(('ep', 'dp')), may hold values from -6 to 6
- grad_out: bfloat16 [32768, 7168], P(('ep', 'dp')), may hold values from -6 to 6
- route_ids: int32 [32768, 8], P(('ep', 'dp')), may hold values from 0 to 255, as said below
- route_probs: float32 [32768, 8], P(('ep', 'dp')), may hold values from 0.1 to 1
- replica_pick: int32 [32768, 8], P(('ep', 'dp')), may hold values from 0 to 1, as said below
- plan: int32 [8], replicated, may hold values from 0 to 5, as said below
- w_gate: bfloat16 [8, 7168, 2048], P('ep', 'dp'), may hold values from -0.0625 to 0.0625
- w_up: bfloat16 [8, 7168, 2048], P('ep', 'dp'), may hold values from -0.0625 to 0.0625
- w_down: bfloat16 [8, 2048, 7168], P('ep', None, 'dp'), may hold values from -0.125 to 0.125
Outputs:
- grad_tokens: bfloat16 [32768, 7168], P(('ep', 'dp'))
- grad_gate: bfloat16 [8, 7168, 2048], P('ep', 'dp')
- grad_up: bfloat16 [8, 7168, 2048], P('ep', 'dp')
- grad_down: bfloat16 [8, 2048, 7168], P('ep', None, 'dp')
Inputs may be any that keep to these rules, and one draw needn't show every extreme that they name: `route_ids`: each row names 8 different experts; ids under 6 are the experts held here, and each of them appears in some row of every block of 256 tokens. `replica_pick`: under this pick no replica receives more than 6 of one device's rows, and in every device's rows some replica receives exactly 6. `plan`: every expert under 6 is held by one or two slots; exactly 2 experts are held by two.
All inputs are finite; a program needn't handle non-finite values.
Results may differ from a plain program's by a relative error of at most 0.029.
Values may be sent and summed in bfloat16 or wider, within the bound.
No kernel may reach another device: no remote copies, remote signals or barrier semaphores. Data moves between devices by JAX's collectives and lax.ppermute only.
A program may use at most 128 MiB of HBM per device.

v0:
```python
import functools
import itertools

import jax
import jax.numpy as jnp
import numpy as np
from jax import lax
from jax.experimental import pallas as pl
from jax.experimental.pallas import tpu as pltpu
from jax.sharding import PartitionSpec as P

MOST = 6
PAD = 8
BLOCK = 256
CONTRACT_ROWS = (((0,), (0,)), ((), ()))
CONTRACT_UNITS = (((1,), (1,)), ((), ()))


def pairings(replicas):
    tables = []
    pairs = list(itertools.combinations(range(replicas), 2))
    for first, second in itertools.combinations(pairs, 2):
        if not set(first) & set(second):
            partner = list(range(replicas))
            for a, b in (first, second):
                partner[a], partner[b] = b, a
            tables.append(partner)
    return tables


def dispatch_kernel(ids_ref, pick_ref, probs_ref, plan_ref, tok_ref, grad_ref, send_ref, sel_ref, scale_ref):
    replicas = plan_ref.shape[0]
    tokens = ids_ref.shape[1]

    @pl.when(pl.program_id(0) == 0)
    def _():
        ids = ids_ref[...]
        pick = pick_ref[...]
        probs = probs_ref[...]
        hits, weights = [], []
        for r in range(replicas):
            expert = plan_ref[r]
            copies = jnp.int32(0)
            rank = jnp.int32(0)
            for other in range(replicas):
                same = (plan_ref[other] == expert).astype(jnp.int32)
                copies += same
                if other < r:
                    rank += same
            wanted = jnp.where(copies > 1, lax.rem(pick, jnp.int32(2)), 0)
            matched = (ids == expert) & (wanted == rank)
            hits.append(jnp.max(jnp.where(matched, 1.0, 0.0), axis=0, keepdims=True))
            weights.append(jnp.sum(jnp.where(matched, probs, 0.0), axis=0, keepdims=True))
        hit = jnp.concatenate(hits, axis=0)
        earlier = lax.broadcasted_iota(jnp.int32, (tokens, tokens), 0) < lax.broadcasted_iota(
            jnp.int32, (tokens, tokens), 1
        )
        before = jnp.dot(
            hit.astype(jnp.bfloat16),
            earlier.astype(jnp.float32).astype(jnp.bfloat16),
            preferred_element_type=jnp.float32,
        )
        slot = lax.broadcasted_iota(jnp.int32, (PAD, tokens), 0).astype(jnp.float32)
        rows, scales = [], []
        for r in range(replicas):
            chosen = jnp.where((before[r : r + 1] == slot) & (hit[r : r + 1] > 0.0), 1.0, 0.0)
            rows.append(chosen)
            scales.append(jnp.sum(chosen * weights[r], axis=1, keepdims=True))
        sel_ref[...] = jnp.concatenate(rows, axis=0).astype(jnp.bfloat16)
        scale_ref[...] = jnp.broadcast_to(jnp.concatenate(scales, axis=0), scale_ref.shape)

    sel = sel_ref[...]
    rows_in = jnp.dot(sel, tok_ref[...], preferred_element_type=jnp.float32)
    rows_grad = jnp.dot(sel, grad_ref[...], preferred_element_type=jnp.float32) * scale_ref[:, :1]
    width = send_ref.shape[3] // 2
    for b in range(send_ref.shape[1]):
        cols = slice(b * width, (b + 1) * width)
        both = jnp.concatenate([rows_in[:, cols], rows_grad[:, cols]], axis=1)
        send_ref[:, b] = both.reshape(replicas, PAD, 2 * width).astype(jnp.bfloat16)


def dispatch(tokens, grad_out, route_ids, route_probs, replica_pick, plan, dp_count):
    count, model_width = tokens.shape
    replicas = plan.shape[0]
    width = model_width // dp_count
    top = route_ids.shape[1]
    small = pl.BlockSpec((top, count), lambda i: (0, 0))
    return pl.pallas_call(
        dispatch_kernel,
        grid=(dp_count // 2,),
        in_specs=[
            small,
            small,
            small,
            pl.BlockSpec(memory_space=pltpu.SMEM),
            pl.BlockSpec((count, 2 * width), lambda i: (0, i)),
            pl.BlockSpec((count, 2 * width), lambda i: (0, i)),
        ],
        out_specs=[
            pl.BlockSpec((replicas, 2, PAD, 2 * width), lambda i: (0, i, 0, 0)),
            pl.BlockSpec((replicas * PAD, count), lambda i: (0, 0)),
        ],
        out_shape=[
            jax.ShapeDtypeStruct((replicas, dp_count, PAD, 2 * width), jnp.bfloat16),
            jax.ShapeDtypeStruct((replicas * PAD, count), jnp.bfloat16),
        ],
        scratch_shapes=[pltpu.VMEM((replicas * PAD, 128), jnp.float32)],
        compiler_params=pltpu.CompilerParams(vmem_limit_bytes=60 * 2**20),
        name="dispatch",
    )(route_ids.T, replica_pick.T, route_probs.T, plan, tokens, grad_out)


def combine_kernel(sel_ref, back_ref, out_ref):
    sel = sel_ref[...]
    parts = []
    for b in range(back_ref.shape[1]):
        rows = back_ref[:, b].astype(jnp.float32).reshape(-1, back_ref.shape[3]).astype(jnp.bfloat16)
        parts.append(lax.dot_general(sel, rows, CONTRACT_ROWS, preferred_element_type=jnp.float32))
    out_ref[...] = jnp.concatenate(parts, axis=1).astype(jnp.bfloat16)


def combine(sel, back):
    slots, count = sel.shape
    replicas, dp_count, pad, width = back.shape
    return pl.pallas_call(
        combine_kernel,
        grid=(dp_count // 2,),
        in_specs=[
            pl.BlockSpec((slots, count), lambda i: (0, 0)),
            pl.BlockSpec((replicas, 2, pad, width), lambda i: (0, i, 0, 0)),
        ],
        out_specs=pl.BlockSpec((count, 2 * width), lambda i: (0, i)),
        out_shape=jax.ShapeDtypeStruct((count, dp_count * width), jnp.bfloat16),
        compiler_params=pltpu.CompilerParams(vmem_limit_bytes=32 * 2**20),
        name="combine",
    )(sel, back)


def added(first, *others):
    total = first.astype(jnp.float32)
    for other in others:
        total = total + other.astype(jnp.float32)
    return total


def backward_units(gate, up_val, hidden_grad):
    sigmoid_gate = jax.nn.sigmoid(gate)
    activated = gate * sigmoid_gate
    hidden = (activated * up_val).astype(jnp.bfloat16)
    up_grad = (hidden_grad * activated).astype(jnp.bfloat16)
    gate_grad = (hidden_grad * up_val * sigmoid_gate * (1.0 + gate * (1.0 - sigmoid_gate))).astype(
        jnp.bfloat16
    )
    return hidden, gate_grad, up_grad


def units_kernel(in_ref, grad_ref, gate_sum, up_sum, down_sum, gate_ref, up_ref, terms_ref, rows_ref, total_ref):
    step = pl.program_id(0)
    hidden, gate_grad, up_grad = backward_units(
        *(part[...].astype(jnp.float32) for part in (gate_sum, up_sum, down_sum))
    )
    for k, (rows, units) in enumerate(((in_ref, gate_grad), (in_ref, up_grad), (grad_ref, hidden))):
        terms_ref[k] = jnp.dot(rows[...], units, preferred_element_type=jnp.float32).astype(jnp.bfloat16)
    part = lax.dot_general(
        gate_grad, gate_ref[...], CONTRACT_UNITS, preferred_element_type=jnp.float32
    ) + lax.dot_general(up_grad, up_ref[...], CONTRACT_UNITS, preferred_element_type=jnp.float32)

    @pl.when(step == 0)
    def _():
        total_ref[...] = part

    @pl.when(step > 0)
    def _():
        total_ref[...] += part

    @pl.when(step == pl.num_programs(0) - 1)
    def _():
        rows_ref[...] = total_ref[...].astype(jnp.bfloat16)


def unit_terms(in_t, grad_t, sums, gate_w, up_w):
    width, rows = in_t.shape
    count = gate_w.shape[1]
    whole = pl.BlockSpec((width, rows), lambda i: (0, 0))
    part = pl.BlockSpec((rows, BLOCK), lambda i: (0, i))
    weight = pl.BlockSpec((width, BLOCK), lambda i: (0, i))
    return pl.pallas_call(
        units_kernel,
        grid=(count // BLOCK,),
        in_specs=[whole, whole, part, part, part, weight, weight],
        out_specs=[
            pl.BlockSpec((3, width, BLOCK), lambda i: (0, 0, i)),
            pl.BlockSpec((rows, width), lambda i: (0, 0)),
        ],
        out_shape=[
            jax.ShapeDtypeStruct((3, width, count), jnp.bfloat16),
            jax.ShapeDtypeStruct((rows, width), jnp.bfloat16),
        ],
        scratch_shapes=[pltpu.VMEM((rows, width), jnp.float32)],
        compiler_params=pltpu.CompilerParams(vmem_limit_bytes=60 * 2**20),
        cost_estimate=pl.CostEstimate(
            flops=10 * rows * width * count, bytes_accessed=20 * 2**20, transcendentals=rows * count
        ),
        name="unit_terms",
    )(in_t, grad_t, *sums, gate_w, up_w)


def which_pairing(plan, tables):
    replicas = plan.shape[0]
    same = (plan[:, None] == plan[None, :]) & ~np.eye(replicas, dtype=bool)
    ids = jnp.arange(replicas, dtype=jnp.int32)
    partner = ids + jnp.sum(jnp.where(same, ids[None, :] - ids[:, None], 0), axis=1)
    agree = jnp.all(jnp.asarray(tables, jnp.int32) == partner[None, :], axis=1)
    return jnp.sum(jnp.where(agree, jnp.arange(len(tables), dtype=jnp.int32), 0))


def from_partner(terms, index, tables):
    def branch(partner, value):
        return lax.ppermute(value, "ep", [(r, p) for r, p in enumerate(partner) if p != r])

    return lax.switch(index, [functools.partial(branch, t) for t in tables], terms)


def on_device(tokens, grad_out, route_ids, route_probs, replica_pick, plan, w_gate, w_up, w_down):
    replicas = plan.shape[0]
    dp_count = lax.axis_size("dp")
    width = tokens.shape[1] // dp_count
    tables = pairings(replicas)
    index = which_pairing(plan, tables)
    send, sel = dispatch(tokens, grad_out, route_ids, route_probs, replica_pick, plan, dp_count)
    recv = lax.all_to_all(
        send.reshape(replicas * dp_count, PAD, 2 * width),
        ("ep", "dp"),
        split_axis=0,
        concat_axis=0,
        tiled=True,
    )
    rows = recv[:, :MOST].reshape(-1, 2 * width)
    rows_in, rows_grad = rows[:, :width], rows[:, width:]
    gate_w, up_w, down_w = w_gate[0], w_up[0], w_down[0]
    sums = lax.psum(
        tuple(
            p.astype(jnp.bfloat16)
            for p in (
                jnp.dot(rows_in, gate_w, preferred_element_type=jnp.float32),
                jnp.dot(rows_in, up_w, preferred_element_type=jnp.float32),
                lax.dot_general(rows_grad, down_w, CONTRACT_UNITS, preferred_element_type=jnp.float32),
            )
        ),
        "dp",
    )
    in_t, grad_t, index, sums = lax.optimization_barrier((rows_in.T, rows_grad.T, index, sums))
    terms, row_grads = unit_terms(in_t, grad_t, sums, gate_w, up_w)
    other = from_partner(terms, index, tables)
    grads = [added(terms[k], other[k]).astype(jnp.bfloat16) for k in range(3)]
    back = row_grads.reshape(replicas * dp_count, MOST, width)
    back = jnp.pad(back, ((0, 0), (0, PAD - MOST), (0, 0)))
    back = lax.all_to_all(back, ("ep", "dp"), split_axis=0, concat_axis=0, tiled=True)
    grad_tokens = combine(sel, back.reshape(replicas, dp_count, PAD, width))
    return grad_tokens, grads[0][None], grads[1][None], grads[2].T[None]


def solution(mesh):
    return jax.shard_map(
        on_device,
        mesh=mesh,
        in_specs=(
            P(("ep", "dp"), None),
            P(("ep", "dp"), None),
            P(("ep", "dp"), None),
            P(("ep", "dp"), None),
            P(("ep", "dp"), None),
            P(),
            P("ep", "dp", None),
            P("ep", "dp", None),
            P("ep", None, "dp"),
        ),
        out_specs=(
            P(("ep", "dp"), None),
            P("ep", "dp", None),
            P("ep", "dp", None),
            P("ep", None, "dp"),
        ),
        check_vma=False,
    )
```

profile of v0, /device:TPU:32, one launch (start us, length us, event | category | flops | bytes accessed | tf_op | source)
XLA Modules:
  0.0 335.1 jit_solution(17141261060764311122)
XLA Ops:
  7.2 0.0 copy-start
  7.2 0.0 all-reduce.4.cloned.1.call-start
  7.2 8.2 %dispatch.1 = (bf16[8,16,8,896]{3,2,1,0:T(8,128)(2,1)}, bf16[64,256]{1,0:T(8,128)(2,1)}) custom-call(s32[8,256]{1,0:T(8,128)} %bitcast.28, s32[8,256]{1,0:T(8,128)} %bitcast.29, f32[8,256]{1,0:T(8,128)} %bitcast.30, s32[8]{0:T(128)} %plan_ref.1, bf16[256,7168]{1,0:T(8,128)(2,1)} %tok_ref.1, bf16[256,7168]{1,0:T(8,128)(2,1)} %grad_ref.1), custom_call_target="tpu_custom_call" | custom-call | tf_op jit(solution)/shard_map/dispatch/pallas_call | solution.py:88
  15.5 37.2 %all_to_all.10 = bf16[128,8,896]{2,1,0:T(8,128)(2,1)} all-to-all(bf16[128,8,896]{2,1,0:T(8,128)(2,1)} %bitcast.25), channel_id=1, replica_groups=mesh['ep'=8,'dp'=16] {'ep','dp'}, dimensions={0} | all-to-all | bytes 3670016 | tf_op jit(solution)/shard_map/all_to_all | solution.py:231
  52.6 3.6 %reshape.33 = bf16[768,896]{1,0:T(8,128)(2,1)} reshape(bf16[128,6,896]{2,1,0:T(8,128)(2,1)} %bitcast.24) | data formatting | bytes 2752512 | tf_op jit(solution)/shard_map/reshape | solution.py:238
  56.2 0.0 copy-done
  56.2 0.0 copy-start.2
  56.2 0.0 copy-start.7
  56.2 4.8 %convolution_convert_fusion = bf16[768,2048]{1,0:T(8,128)(2,1)} fusion(bf16[1,2048,448]{1,2,0:T(8,128)(2,1)S(1)} %copy-done, bf16[768,896]{1,0:T(8,128)(2,1)} %reshape.33), kind=kOutput, calls=%fused_computation.3 | convolution fusion | flops 1410859008 | bytes 5767168 | tf_op jit(solution)/shard_map/dot_general | solution.py:247
  61.0 0.0 copy-done.2
  61.0 0.0 copy-done.7
  61.0 0.0 copy-start.6
  61.0 3.5 %convolution_convert_fusion.1 = bf16[768,2048]{1,0:T(8,128)(2,1)} fusion(bf16[1,448,2048]{2,1,0:T(8,128)(2,1)S(1)} %copy-done.7, bf16[768,896]{1,0:T(8,128)(2,1)S(1)} %copy-done.2), kind=kOutput, calls=%fused_computation.4 | convolution fusion | flops 1410859008 | bytes 5767168 | tf_op jit(solution)/shard_map/dot_general | solution.py:246
  64.5 0.0 copy-done.6
  64.5 3.5 %convolution_convert_fusion.2 = bf16[768,2048]{1,0:T(8,128)(2,1)} fusion(bf16[1,448,2048]{2,1,0:T(8,128)(2,1)S(1)} %copy-done.6, bf16[768,896]{1,0:T(8,128)(2,1)S(1)} %copy-done.2), kind=kOutput, calls=%fused_computation.5 | convolution fusion | flops 1410859008 | bytes 5767168 | tf_op jit(solution)/shard_map/dot_general | solution.py:245
  67.9 0.0 copy-start.4
  67.9 0.0 copy-start.5
  67.9 0.0 copy-start.3
  67.9 0.0 all-reduce.4.cloned.1.call-update
  67.9 0.6 copy-done.4
  68.6 0.0 copy-done.5
  68.6 0.2 select_reduce_fusion
  68.8 0.0 copy-done.3
  68.8 0.1 compare_reduce_fusion
  68.9 0.6 select_reduce_fusion.1
  69.5 2.6 fusion.7
  72.1 2.4 copy.20
  74.5 1.1 copy.21
  75.6 139.9 %all-reduce.4.cloned.1.call-done = (bf16[768,2048]{1,0:T(8,128)(2,1)}, bf16[768,2048]{1,0:T(8,128)(2,1)}, bf16[768,2048]{1,0:T(8,128)(2,1)}) async-done(((bf16[768,2048]{1,0:T(8,128)(2,1)}, bf16[768,2048]{1,0:T(8,128)(2,1)}, bf16[768,2048]{1,0:T(8,128)(2,1)}), (bf16[768,2048]{1,0:T(8,128)(2,1)}, bf16[768,2048]{1,0:T(8,128)(2,1)}, bf16[768,2048]{1,0:T(8,128)(2,1)})) %all-reduce.4.cloned.1.call-update) | async-done | bytes 9437200 | tf_op jit(solution)/shard_map/psum | solution.py:241
  215.6 15.3 %unit_terms.1 = (bf16[3,448,2048]{2,1,0:T(8,128)(2,1)}, bf16[768,448]{1,0:T(8,128)(2,1)}) custom-call(bf16[448,768]{1,0:T(8,128)(2,1)} %bitcast.26, bf16[448,768]{1,0:T(8,128)(2,1)} %bitcast.27, bf16[768,2048]{1,0:T(8,128)(2,1)} %get-tuple-element.439.gate_sum, bf16[768,2048]{1,0:T(8,128)(2,1)} %get-tuple-element.440.up_sum, ...), custom_call_target="tpu_custom_call" | custom-call | flops 7046430720 | bytes 20971520 | tf_op jit(solution)/shard_map/unit_terms/pallas_call | solution.py:187
  230.9 1.5 reshape.34
  232.4 1.2 pad.4
  233.6 7.2 %all-to-all-start.1 = ((bf16[128,8,448]{2,1,0:T(8,128)(2,1)}), bf16[128,8,448]{2,1,0:T(8,128)(2,1)S(1)}, u32[]{:S(2)}, u32[]{:S(2)}) async-start(bf16[128,8,448]{2,1,0:T(8,128)(2,1)} %pad.4), calls=%async_computation.1 | async-start | bytes 2097152 | tf_op jit(solution)/shard_map/all_to_all | solution.py:258
  241.4 74.9 %conditional.1 = (bf16[3,448,2048]{2,1,0:T(8,128)(2,1)}) conditional(s32[]{:T(128)} %clamp.3, bf16[3,448,2048]{2,1,0:T(8,128)(2,1)} %get-tuple-element.443, bf16[3,448,2048]{2,1,0:T(8,128)(2,1)} %get-tuple-element.443, bf16[3,448,2048]{2,1,0:T(8,128)(2,1)} %get-tuple-element.443, ...), branch_computations={%region_6.7_spmd, %region_7.8_spmd, %region_8.9_spmd, %region_9.10... | conditional | bytes 22020144 | solution.py:221
  241.7 10.2 %collective-permute-start.182 = (bf16[3,448,2048]{2,1,0:T(8,128)(2,1)}, bf16[3,448,2048]{2,1,0:T(8,128)(2,1)}, u32[]{:S(2)}, u32[]{:S(2)}) collective-permute-start(bf16[3,448,2048]{2,1,0:T(8,128)(2,1)} %param.182), channel_id=1, source_target_pairs={{32,80},{80,32},{96,112},{112,96},{33,81},{81,33},{97,113},{113,97... | collective-permute-start | bytes 16515080 | tf_op jit(solution)/shard_map/cond/branch_182_fun/ppermute | solution.py:219
  251.9 64.4 %collective-permute-done.182 = bf16[3,448,2048]{2,1,0:T(8,128)(2,1)} collective-permute-done((bf16[3,448,2048]{2,1,0:T(8,128)(2,1)}, bf16[3,448,2048]{2,1,0:T(8,128)(2,1)}, u32[]{:S(2)}, u32[]{:S(2)}) %collective-permute-start.182) | collective-permute-done | bytes 5505056 | tf_op jit(solution)/shard_map/cond/branch_182_fun/ppermute | solution.py:219
  316.3 0.0 copy-start.1
  316.3 6.8 %fusion = (bf16[1,2048,448]{1,2,0:T(8,128)(2,1)}, bf16[1,448,2048]{2,1,0:T(8,128)(2,1)}, bf16[1,448,2048]{2,1,0:T(8,128)(2,1)}) fusion(bf16[3,448,2048]{2,1,0:T(8,128)(2,1)} %get-tuple-element.456, bf16[3,448,2048]{2,1,0:T(8,128)(2,1)} %get-tuple-element.443), kind=kLoop, calls=%fused_computation.6 | loop fusion | flops 11010048 | bytes 16515072 | tf_op jit(solution)/shard_map/broadcast_in_dim | solution.py:260
  323.1 0.0 all-to-all-done.1
  323.1 0.0 copy-done.1
  323.1 5.1 %combine.1 = bf16[256,7168]{1,0:T(8,128)(2,1)} custom-call(bf16[64,256]{1,0:T(8,128)(2,1)S(1)} %copy-done.1, bf16[8,16,8,448]{3,2,1,0:T(8,128)(2,1)S(1)} %bitcast.23), custom_call_target="tpu_custom_call" | custom-call | tf_op jit(solution)/shard_map/combine/pallas_call | solution.py:125
  (1 shorter events, 0.0 us)
Async XLA Ops:
  7.2 49.0 %copy-start = (bf16[1,2048,448]{1,2,0:T(8,128)(2,1)S(1)}, bf16[1,2048,448]{1,2,0:T(8,128)(2,1)}, u32[]{:S(2)}) copy-start(bf16[1,2048,448]{1,2,0:T(8,128)(2,1)} %param.229) | copy-start | bytes 5505028
  7.2 208.4 %all-reduce.4.cloned.1.call-start = ((), (), s32[]{:S(2)}) async-start(), calls=%async_computation.2 | async-start | bytes 18874368 | tf_op jit(solution)/shard_map/psum | solution.py:241
  56.2 4.8 %copy-start.2 = (bf16[768,896]{1,0:T(8,128)(2,1)S(1)}, bf16[768,896]{1,0:T(8,128)(2,1)}, u32[]{:S(2)}) copy-start(bf16[768,896]{1,0:T(8,128)(2,1)} %reshape.33) | copy-start | bytes 4128772
  56.2 4.8 %copy-start.7 = (bf16[1,448,2048]{2,1,0:T(8,128)(2,1)S(1)}, bf16[1,448,2048]{2,1,0:T(8,128)(2,1)}, u32[]{:S(2)}) copy-start(bf16[1,448,2048]{2,1,0:T(8,128)(2,1)} %param.228) | copy-start | bytes 5505028
  61.0 3.5 %copy-start.6 = (bf16[1,448,2048]{2,1,0:T(8,128)(2,1)S(1)}, bf16[1,448,2048]{2,1,0:T(8,128)(2,1)}, u32[]{:S(2)}) copy-start(bf16[1,448,2048]{2,1,0:T(8,128)(2,1)} %param.227) | copy-start | bytes 5505028
  67.9 0.7 copy-start.4
  67.9 0.7 copy-start.5
  67.9 0.9 copy-start.3
  233.6 89.5 %all-to-all-start.1 = ((bf16[128,8,448]{2,1,0:T(8,128)(2,1)}), bf16[128,8,448]{2,1,0:T(8,128)(2,1)S(1)}, u32[]{:S(2)}, u32[]{:S(2)}) async-start(bf16[128,8,448]{2,1,0:T(8,128)(2,1)} %pad.4), calls=%async_computation.1 | async-start | bytes 2097152 | tf_op jit(solution)/shard_map/all_to_all | solution.py:258
  241.7 74.6 %collective-permute-start.182 = (bf16[3,448,2048]{2,1,0:T(8,128)(2,1)}, bf16[3,448,2048]{2,1,0:T(8,128)(2,1)}, u32[]{:S(2)}, u32[]{:S(2)}) collective-permute-start(bf16[3,448,2048]{2,1,0:T(8,128)(2,1)} %param.182), channel_id=1, source_target_pairs={{32,80},{80,32},{96,112},{112,96},{33,81},{81,33},{97,113},{113,97... | collective-permute-start | bytes 16515080 | tf_op jit(solution)/shard_map/cond/branch_182_fun/ppermute | solution.py:219
  316.3 6.8 %copy-start.1 = (bf16[64,256]{1,0:T(8,128)(2,1)S(1)}, bf16[64,256]{1,0:T(8,128)(2,1)}, u32[]{:S(2)}) copy-start(bf16[64,256]{1,0:T(8,128)(2,1)} %get-tuple-element.435.sel_ref) | copy-start | bytes 98308
Sparse Core Ops, SparseCore 0:
  68.1 147.4 all-reduce.3
where the time goes:
time: 337 us; the launch traced here: 335 us
  waiting for transfers between devices  204 us (61%)
  blocking collectives  37.2 us (11%)
  Pallas kernels  28.7 us (9%)
  starting transfers between devices  17.4 us (5%)
  between operations  14.7 us (4%)
  local copies, waits for them, and re-layouts  13.1 us (4%)
  matrix products  11.7 us (3%)
  other arithmetic  7.74 us (2%)
    psum x1, waiting for transfers between devices, on_device(): lax.psum(tuple((p.astype(jnp.bfloat16) for p in (jnp.dot(rows_in, gate_w,...  140 us
    ppermute x1, waiting for transfers between devices, branch(): lax.ppermute(value, 'ep', [(r, p) for r, p in enumerate(partner) if p != r])  64.4 us
    all_to_all x1, blocking collectives, on_device(): lax.all_to_all(send.reshape(replicas * dp_count, PAD, 2 * width), ('ep',...  37.2 us
    pallas_call x1, Pallas kernels, unit_terms(): pl.pallas_call(units_kernel, grid=(count // BLOCK,), in_specs=[whole, who...  15.3 us
    ppermute x1, starting transfers between devices, branch(): lax.ppermute(value, 'ep', [(r, p) for r, p in enumerate(partner) if p != r])  10.2 us
    pallas_call x1, Pallas kernels, dispatch(): pl.pallas_call(dispatch_kernel, grid=(dp_count // 2,), in_specs=[small, s...  8.24 us
    all_to_all x1, starting transfers between devices, on_device(): lax.all_to_all(back, ('ep', 'dp'), split_axis=0, concat_axis=0, tiled=True)  7.21 us
    broadcast_in_dim x1, other arithmetic, on_device(): return (grad_tokens, grads[0][None], grads[1][None], grads[2].T[None])  6.83 us
  transfers between devices with their start and end apart: 3, of which 2 were waited for; matrix products, arithmetic and copies ran while one was open for 4% of the time, Pallas kernels for 0%

commit v1 on v0

--- a/solution.py
+++ b/solution.py
@@ -12,6 +12,7 @@
 MOST = 6
 PAD = 8
 BLOCK = 256
+CORES = 2
 CONTRACT_ROWS = (((0,), (0,)), ((), ()))
 CONTRACT_UNITS = (((1,), (1,)), ((), ()))
 
@@ -214,11 +215,34 @@
     return jnp.sum(jnp.where(agree, jnp.arange(len(tables), dtype=jnp.int32), 0))
 
 
+def swapped(partner, terms):
+    count = len(partner)
+    chips = count // CORES
+
+    def apart(a, b):
+        steps = (b // CORES - a // CORES) % chips
+        return min(steps, chips - steps)
+
+    def moved(value, pairs):
+        return lax.ppermute(value, "ep", pairs)
+
+    pairs = [(r, p) for r, p in enumerate(partner) if p != r]
+    far = [(r, p) for r, p in pairs if apart(r, p) > 1]
+    near = [(r, p) for r, p in pairs if apart(r, p) <= 1]
+    if len(far) != 2 or all(apart(r, p) == 0 for r, p in near):
+        return moved(terms, pairs)
+    way = -CORES if far[0][0] // CORES % 2 == 0 else CORES
+    first = [(r, (r + way) % count) for r, _ in far]
+    second = [((r + way) % count, p) for r, p in far]
+    flat = terms.reshape(-1, terms.shape[2])
+    cut = flat.shape[0] // 7 * 3
+    upper, lower = flat[:cut], flat[cut:]
+    relayed = moved(moved(lower, first), second) + moved(lower, near)
+    return jnp.concatenate([moved(upper, pairs), relayed], axis=0).reshape(terms.shape)
+
+
 def from_partner(terms, index, tables):
-    def branch(partner, value):
-        return lax.ppermute(value, "ep", [(r, p) for r, p in enumerate(partner) if p != r])
-
-    return lax.switch(index, [functools.partial(branch, t) for t in tables], terms)
+    return lax.switch(index, [functools.partial(swapped, t) for t in tables], terms)
 
 
 def on_device(tokens, grad_out, route_ids, route_probs, replica_pick, plan, w_gate, w_up, w_down):

time: 337 us -> 430 us (1.28)
  the two profiles are of different devices: /device:TPU:32 before, /device:TPU:1 now
where the time goes in v1:
time: 430 us; the launch traced here: 428 us
  waiting for transfers between devices  236 us (55%)
  loops' own time  47 us (11%)
  blocking collectives  38.5 us (9%)
  Pallas kernels  30.7 us (7%)
  starting transfers between devices  26.2 us (6%)
  between operations  14.9 us (3%)
  local copies, waits for them, and re-layouts  12.6 us (3%)
  other arithmetic  12.1 us (3%)
  matrix products  10.5 us (2%)
    psum x1, waiting for transfers between devices, on_device(): lax.psum(tuple((p.astype(jnp.bfloat16) for p in (jnp.dot(rows_in, gate_w,...  143 us
    ppermute x4, waiting for transfers between devices, moved(): return lax.ppermute(value, 'ep', pairs)  93.2 us
    another operation x1, loops' own time, from_partner(): lax.switch(index, [functools.partial(swapped, t) for t in tables], terms)  47 us
    all_to_all x1, blocking collectives, on_device(): lax.all_to_all(send.reshape(replicas * dp_count, PAD, 2 * width), ('ep',...  38.5 us
    ppermute x4, starting transfers between devices, moved(): return lax.ppermute(value, 'ep', pairs)  17.8 us
    pallas_call x1, Pallas kernels, unit_terms(): pl.pallas_call(units_kernel, grid=(count // BLOCK,), in_specs=[whole, who...  15.3 us
  transfers between devices with their start and end apart: 6, of which 4 were waited for; matrix products, arithmetic and copies ran while one was open for 4% of the time, Pallas kernels for 0%

profile of v1, /device:TPU:1, one launch (start us, length us, event | category | flops | bytes accessed | tf_op | source)
XLA Modules:
  0.0 428.4 jit_solution(16515287499880280481)
XLA Ops:
  7.2 0.0 copy-start
  7.2 0.0 all-reduce.4.cloned.1.call-start
  7.2 8.2 %dispatch.1 = (bf16[8,16,8,896]{3,2,1,0:T(8,128)(2,1)}, bf16[64,256]{1,0:T(8,128)(2,1)}) custom-call(s32[8,256]{1,0:T(8,128)} %bitcast.283, s32[8,256]{1,0:T(8,128)} %bitcast.284, f32[8,256]{1,0:T(8,128)} %bitcast.285, s32[8]{0:T(128)} %plan_ref.1, bf16[256,7168]{1,0:T(8,128)(2,1)} %tok_ref.1, bf16[256,7168]{1,0:T(8,128)(2,1)} %grad_ref.1), custom_call_target="tpu_custom_call" | custom-call | tf_op jit(solution)/shard_map/dispatch/pallas_call | solution.py:89
  15.5 38.5 %all_to_all.10 = bf16[128,8,896]{2,1,0:T(8,128)(2,1)} all-to-all(bf16[128,8,896]{2,1,0:T(8,128)(2,1)} %bitcast.280), channel_id=1, replica_groups=mesh['ep'=8,'dp'=16] {'ep','dp'}, dimensions={0} | all-to-all | bytes 3670016 | tf_op jit(solution)/shard_map/all_to_all | solution.py:255
  54.0 2.5 reshape.417
  56.5 0.0 copy-done
  56.5 0.0 copy-start.7
  56.5 3.5 convolution_convert_fusion
  60.0 0.0 copy-done.7
  60.0 0.0 copy-start.6
  60.0 3.5 convolution_convert_fusion.1
  63.6 0.0 copy-done.6
  63.6 3.5 convolution_convert_fusion.2
  67.0 0.0 copy-start.4
  67.0 0.0 copy-start.5
  67.0 0.0 copy-start.3
  67.0 0.0 all-reduce.4.cloned.1.call-update
  67.0 0.6 copy-done.4
  67.7 0.0 copy-done.5
  67.7 0.2 select_reduce_fusion
  67.9 0.0 copy-done.3
  67.9 0.1 compare_reduce_fusion
  68.0 0.6 select_reduce_fusion.1
  68.6 0.4 fusion.7
  69.0 1.1 copy.20
  70.1 1.1 copy.21
  71.2 142.7 %all-reduce.4.cloned.1.call-done = (bf16[768,2048]{1,0:T(8,128)(2,1)}, bf16[768,2048]{1,0:T(8,128)(2,1)}, bf16[768,2048]{1,0:T(8,128)(2,1)}) async-done(((bf16[768,2048]{1,0:T(8,128)(2,1)}, bf16[768,2048]{1,0:T(8,128)(2,1)}, bf16[768,2048]{1,0:T(8,128)(2,1)}), (bf16[768,2048]{1,0:T(8,128)(2,1)}, bf16[768,2048]{1,0:T(8,128)(2,1)}, bf16[768,2048]{1,0:T(8,128)(2,1)})) %all-reduce.4.cloned.1.call-update) | async-done | bytes 9437200 | tf_op jit(solution)/shard_map/psum | solution.py:265
  213.9 15.3 %unit_terms.1 = (bf16[3,448,2048]{2,1,0:T(8,128)(2,1)}, bf16[768,448]{1,0:T(8,128)(2,1)}) custom-call(bf16[448,768]{1,0:T(8,128)(2,1)} %bitcast.281, bf16[448,768]{1,0:T(8,128)(2,1)} %bitcast.282, bf16[768,2048]{1,0:T(8,128)(2,1)} %get-tuple-element.439.gate_sum, bf16[768,2048]{1,0:T(8,128)(2,1)} %get-tuple-element.440.up_sum, ...), custom_call_target="tpu_custom_call" | custom-call | flops 7046430720 | bytes 20971520 | tf_op jit(solution)/shard_map/unit_terms/pallas_call | solution.py:188
  229.2 1.5 reshape.418
  230.8 1.2 pad.4
  231.9 8.3 %all-to-all-start.1 = ((bf16[128,8,448]{2,1,0:T(8,128)(2,1)}), bf16[128,8,448]{2,1,0:T(8,128)(2,1)}, u32[]{:S(2)}, u32[]{:S(2)}) async-start(bf16[128,8,448]{2,1,0:T(8,128)(2,1)} %pad.4), calls=%async_computation.1 | async-start | bytes 2097152 | tf_op jit(solution)/shard_map/all_to_all | solution.py:282
  240.9 166.4 %conditional.1 = (bf16[3,448,2048]{2,1,0:T(8,128)(2,1)}) conditional(s32[]{:T(128)} %clamp.3, bf16[3,448,2048]{2,1,0:T(8,128)(2,1)} %get-tuple-element.443, bf16[3,448,2048]{2,1,0:T(8,128)(2,1)} %get-tuple-element.443, bf16[3,448,2048]{2,1,0:T(8,128)(2,1)} %get-tuple-element.443, ...), branch_computations={%region_6.7_spmd, %region_7.8_spmd, %region_8.9_spmd, %region_9.10... | conditional | flops 12582912 | bytes 78643368 | solution.py:245
  263.2 2.3 slice.471
  265.5 5.4 %collective-permute-start.247 = (bf16[768,2048]{1,0:T(8,128)(2,1)S(1)}, bf16[768,2048]{1,0:T(8,128)(2,1)S(1)}, u32[]{:S(2)}, u32[]{:S(2)}) collective-permute-start(bf16[768,2048]{1,0:T(8,128)(2,1)S(1)} %slice.471), channel_id=1, source_target_pairs={{16,112},{80,48},{17,113},{81,49},{18,114},{82,50},{19,115},{83,51... | collective-permute-start | bytes 9437192 | tf_op jit(solution)/shard_map/cond/branch_78_fun/ppermute | solution.py:227
  270.8 0.9 collective-permute-start.249
  271.7 65.1 %collective-permute-done.247 = bf16[768,2048]{1,0:T(8,128)(2,1)S(1)} collective-permute-done((bf16[768,2048]{1,0:T(8,128)(2,1)S(1)}, bf16[768,2048]{1,0:T(8,128)(2,1)S(1)}, u32[]{:S(2)}, u32[]{:S(2)}) %collective-permute-start.247) | collective-permute-done | bytes 3145760 | tf_op jit(solution)/shard_map/cond/branch_78_fun/ppermute | solution.py:227
  336.8 1.3 collective-permute-start.248
  338.1 1.8 slice.470
  339.9 10.3 %collective-permute-start.246 = (bf16[576,2048]{1,0:T(8,128)(2,1)S(1)}, bf16[576,2048]{1,0:T(8,128)(2,1)S(1)}, u32[]{:S(2)}, u32[]{:S(2)}) collective-permute-start(bf16[576,2048]{1,0:T(8,128)(2,1)S(1)} %slice.470), channel_id=1, source_target_pairs={{0,96},{16,80},{80,16},{96,0},{1,97},{17,81},{81,17},{97,1},{2,98}... | collective-permute-start | bytes 7077896 | tf_op jit(solution)/shard_map/cond/branch_78_fun/ppermute | solution.py:227
  350.2 0.0 collective-permute-done.249
  350.2 24.9 %collective-permute-done.248 = bf16[768,2048]{1,0:T(8,128)(2,1)S(1)} collective-permute-done((bf16[768,2048]{1,0:T(8,128)(2,1)S(1)}, bf16[768,2048]{1,0:T(8,128)(2,1)S(1)}, u32[]{:S(2)}, u32[]{:S(2)}) %collective-permute-start.248) | collective-permute-done | bytes 3145760 | tf_op jit(solution)/shard_map/cond/branch_78_fun/ppermute | solution.py:227
  375.1 1.4 add.174
  376.5 3.3 collective-permute-done.246
  379.8 2.8 pad_maximum_fusion.25
  407.2 0.0 copy-start.2
  407.3 0.0 copy-start.1
  407.3 6.9 %fusion = (bf16[1,2048,448]{1,2,0:T(8,128)(2,1)}, bf16[1,448,2048]{2,1,0:T(8,128)(2,1)}, bf16[1,448,2048]{2,1,0:T(8,128)(2,1)}) fusion(bf16[3,448,2048]{2,1,0:T(8,128)(2,1)} %get-tuple-element.456, bf16[3,448,2048]{2,1,0:T(8,128)(2,1)} %get-tuple-element.443), kind=kLoop, calls=%fused_computation.70 | loop fusion | flops 11010048 | bytes 16515072 | tf_op jit(solution)/shard_map/broadcast_in_dim | solution.py:284
  414.2 0.0 all-to-all-done.1
  414.2 0.0 copy-done.2
  414.2 7.1 %combine.1 = bf16[256,7168]{1,0:T(8,128)(2,1)} custom-call(bf16[64,256]{1,0:T(8,128)(2,1)S(1)} %copy-done.2, bf16[8,16,8,448]{3,2,1,0:T(8,128)(2,1)} %bitcast.137.back_ref), custom_call_target="tpu_custom_call" | custom-call | tf_op jit(solution)/shard_map/combine/pallas_call | solution.py:126
  421.3 0.0 copy-done.1
  (1 shorter events, 0.0 us)
Async XLA Ops:
  7.2 49.3 %copy-start = (bf16[1,2048,448]{1,2,0:T(8,128)(2,1)S(1)}, bf16[1,2048,448]{1,2,0:T(8,128)(2,1)}, u32[]{:S(2)}) copy-start(bf16[1,2048,448]{1,2,0:T(8,128)(2,1)} %param.229) | copy-start | bytes 5505028
  7.2 206.7 %all-reduce.4.cloned.1.call-start = ((), (), s32[]{:S(2)}) async-start(), calls=%async_computation.2 | async-start | bytes 18874368 | tf_op jit(solution)/shard_map/psum | solution.py:265
  56.5 3.5 copy-start.7
  60.0 3.5 copy-start.6
  67.0 0.7 copy-start.4
  67.0 0.7 copy-start.5
  67.0 0.9 copy-start.3
  231.9 182.3 %all-to-all-start.1 = ((bf16[128,8,448]{2,1,0:T(8,128)(2,1)}), bf16[128,8,448]{2,1,0:T(8,128)(2,1)}, u32[]{:S(2)}, u32[]{:S(2)}) async-start(bf16[128,8,448]{2,1,0:T(8,128)(2,1)} %pad.4), calls=%async_computation.1 | async-start | bytes 2097152 | tf_op jit(solution)/shard_map/all_to_all | solution.py:282
  265.5 71.3 %collective-permute-start.247 = (bf16[768,2048]{1,0:T(8,128)(2,1)S(1)}, bf16[768,2048]{1,0:T(8,128)(2,1)S(1)}, u32[]{:S(2)}, u32[]{:S(2)}) collective-permute-start(bf16[768,2048]{1,0:T(8,128)(2,1)S(1)} %slice.471), channel_id=1, source_target_pairs={{16,112},{80,48},{17,113},{81,49},{18,114},{82,50},{19,115},{83,51... | collective-permute-start | bytes 9437192 | tf_op jit(solution)/shard_map/cond/branch_78_fun/ppermute | solution.py:227
  270.8 79.3 %collective-permute-start.249 = (bf16[768,2048]{1,0:T(8,128)(2,1)S(1)}, bf16[768,2048]{1,0:T(8,128)(2,1)S(1)}, u32[]{:S(2)}, u32[]{:S(2)}) collective-permute-start(bf16[768,2048]{1,0:T(8,128)(2,1)S(1)} %slice.471), channel_id=1, source_target_pairs={{0,96},{96,0},{1,97},{97,1},{2,98},{98,2},{3,99},{99,3},{4,100},{1... | collective-permute-start | bytes 9437192 | tf_op jit(solution)/shard_map/cond/branch_78_fun/ppermute | solution.py:227
  336.8 38.3 %collective-permute-start.248 = (bf16[768,2048]{1,0:T(8,128)(2,1)S(1)}, bf16[768,2048]{1,0:T(8,128)(2,1)S(1)}, u32[]{:S(2)}, u32[]{:S(2)}) collective-permute-start(bf16[768,2048]{1,0:T(8,128)(2,1)S(1)} %collective-permute-done.247), channel_id=1, source_target_pairs={{112,80},{48,16},{113,81},{49,17},{114,82},{50,18},{115,83},{51,19... | collective-permute-start | bytes 9437192 | tf_op jit(solution)/shard_map/cond/branch_78_fun/ppermute | solution.py:227
  339.9 39.9 %collective-permute-start.246 = (bf16[576,2048]{1,0:T(8,128)(2,1)S(1)}, bf16[576,2048]{1,0:T(8,128)(2,1)S(1)}, u32[]{:S(2)}, u32[]{:S(2)}) collective-permute-start(bf16[576,2048]{1,0:T(8,128)(2,1)S(1)} %slice.470), channel_id=1, source_target_pairs={{0,96},{16,80},{80,16},{96,0},{1,97},{17,81},{81,17},{97,1},{2,98}... | collective-permute-start | bytes 7077896 | tf_op jit(solution)/shard_map/cond/branch_78_fun/ppermute | solution.py:227
  407.2 7.0 %copy-start.2 = (bf16[64,256]{1,0:T(8,128)(2,1)S(1)}, bf16[64,256]{1,0:T(8,128)(2,1)}, u32[]{:S(2)}) copy-start(bf16[64,256]{1,0:T(8,128)(2,1)} %get-tuple-element.435.sel_ref) | copy-start | bytes 98308
  407.3 14.1 %copy-start.1 = (bf16[1,2048,448]{1,2,0:T(8,128)(2,1)S(1)}, bf16[1,2048,448]{1,2,0:T(8,128)(2,1)}, u32[]{:S(2)}) copy-start(bf16[1,2048,448]{1,2,0:T(8,128)(2,1)} %param.229) | copy-start | bytes 5505028
Sparse Core Ops, SparseCore 0:
  67.2 146.6 all-reduce.3

commit v2 on v0

--- a/solution.py
+++ b/solution.py
@@ -84,20 +84,21 @@
     replicas = plan.shape[0]
     width = model_width // dp_count
     top = route_ids.shape[1]
+    step = dp_count // 4
     small = pl.BlockSpec((top, count), lambda i: (0, 0))
     return pl.pallas_call(
         dispatch_kernel,
-        grid=(dp_count // 2,),
+        grid=(dp_count // step,),
         in_specs=[
             small,
             small,
             small,
             pl.BlockSpec(memory_space=pltpu.SMEM),
-            pl.BlockSpec((count, 2 * width), lambda i: (0, i)),
-            pl.BlockSpec((count, 2 * width), lambda i: (0, i)),
+            pl.BlockSpec((count, step * width), lambda i: (0, i)),
+            pl.BlockSpec((count, step * width), lambda i: (0, i)),
         ],
         out_specs=[
-            pl.BlockSpec((replicas, 2, PAD, 2 * width), lambda i: (0, i, 0, 0)),
+            pl.BlockSpec((replicas, step, PAD, 2 * width), lambda i: (0, i, 0, 0)),
             pl.BlockSpec((replicas * PAD, count), lambda i: (0, 0)),
         ],
         out_shape=[
@@ -122,14 +123,15 @@
 def combine(sel, back):
     slots, count = sel.shape
     replicas, dp_count, pad, width = back.shape
+    step = dp_count // 2
     return pl.pallas_call(
         combine_kernel,
-        grid=(dp_count // 2,),
+        grid=(dp_count // step,),
         in_specs=[
             pl.BlockSpec((slots, count), lambda i: (0, 0)),
-            pl.BlockSpec((replicas, 2, pad, width), lambda i: (0, i, 0, 0)),
-        ],
-        out_specs=pl.BlockSpec((count, 2 * width), lambda i: (0, i)),
+            pl.BlockSpec((replicas, step, pad, width), lambda i: (0, i, 0, 0)),
+        ],
+        out_specs=pl.BlockSpec((count, step * width), lambda i: (0, i)),
         out_shape=jax.ShapeDtypeStruct((count, dp_count * width), jnp.bfloat16),
         compiler_params=pltpu.CompilerParams(vmem_limit_bytes=32 * 2**20),
         name="combine",

time: 337 us -> 332 us (0.985)
  the two profiles are of different devices: /device:TPU:32 before, /device:TPU:1 now
where the time goes in v2:
time: 332 us; the launch traced here: 331 us
  waiting for transfers between devices  203 us (61%)
  blocking collectives  38.5 us (12%)
  Pallas kernels  24.5 us (7%)
  starting transfers between devices  18.1 us (5%)
  between operations  14.7 us (4%)
  local copies, waits for them, and re-layouts  13.1 us (4%)
  matrix products  11.7 us (4%)
  other arithmetic  7.74 us (2%)
    psum x1, waiting for transfers between devices, on_device(): lax.psum(tuple((p.astype(jnp.bfloat16) for p in (jnp.dot(rows_in, gate_w,...  139 us
    ppermute x1, waiting for transfers between devices, branch(): lax.ppermute(value, 'ep', [(r, p) for r, p in enumerate(partner) if p != r])  63.7 us
    all_to_all x1, blocking collectives, on_device(): lax.all_to_all(send.reshape(replicas * dp_count, PAD, 2 * width), ('ep',...  38.5 us
    pallas_call x1, Pallas kernels, unit_terms(): pl.pallas_call(units_kernel, grid=(count // BLOCK,), in_specs=[whole, who...  15.3 us
    ppermute x1, starting transfers between devices, branch(): lax.ppermute(value, 'ep', [(r, p) for r, p in enumerate(partner) if p != r])  10.2 us
    all_to_all x1, starting transfers between devices, on_device(): lax.all_to_all(back, ('ep', 'dp'), split_axis=0, concat_axis=0, tiled=True)  7.88 us
    unnamed x19, local copies, waits for them, and re-layouts  6.83 us
    broadcast_in_dim x1, other arithmetic, on_device(): return (grad_tokens, grads[0][None], grads[1][None], grads[2].T[None])  6.83 us
  transfers between devices with their start and end apart: 3, of which 2 were waited for; matrix products, arithmetic and copies ran while one was open for 4% of the time, Pallas kernels for 0%

profile of v2, /device:TPU:1, one launch (start us, length us, event | category | flops | bytes accessed | tf_op | source)
XLA Modules:
  0.0 331.4 jit_solution(10717564339067702246)
XLA Ops:
  7.2 0.0 copy-start
  7.2 0.0 all-reduce.4.cloned.1.call-start
  7.2 6.3 %dispatch.1 = (bf16[8,16,8,896]{3,2,1,0:T(8,128)(2,1)}, bf16[64,256]{1,0:T(8,128)(2,1)}) custom-call(s32[8,256]{1,0:T(8,128)} %bitcast.28, s32[8,256]{1,0:T(8,128)} %bitcast.29, f32[8,256]{1,0:T(8,128)} %bitcast.30, s32[8]{0:T(128)} %plan_ref.1, bf16[256,7168]{1,0:T(8,128)(2,1)} %tok_ref.1, bf16[256,7168]{1,0:T(8,128)(2,1)} %grad_ref.1), custom_call_target="tpu_custom_call" | custom-call | tf_op jit(solution)/shard_map/dispatch/pallas_call | solution.py:89
  13.5 38.5 %all_to_all.10 = bf16[128,8,896]{2,1,0:T(8,128)(2,1)} all-to-all(bf16[128,8,896]{2,1,0:T(8,128)(2,1)} %bitcast.25), channel_id=1, replica_groups=mesh['ep'=8,'dp'=16] {'ep','dp'}, dimensions={0} | all-to-all | bytes 3670016 | tf_op jit(solution)/shard_map/all_to_all | solution.py:233
  52.0 3.6 %reshape.33 = bf16[768,896]{1,0:T(8,128)(2,1)} reshape(bf16[128,6,896]{2,1,0:T(8,128)(2,1)} %bitcast.24) | data formatting | bytes 2752512 | tf_op jit(solution)/shard_map/reshape | solution.py:240
  55.6 0.0 copy-done
  55.6 0.0 copy-start.2
  55.6 0.0 copy-start.7
  55.6 4.8 %convolution_convert_fusion = bf16[768,2048]{1,0:T(8,128)(2,1)} fusion(bf16[1,2048,448]{1,2,0:T(8,128)(2,1)S(1)} %copy-done, bf16[768,896]{1,0:T(8,128)(2,1)} %reshape.33), kind=kOutput, calls=%fused_computation.3 | convolution fusion | flops 1410859008 | bytes 5767168 | tf_op jit(solution)/shard_map/dot_general | solution.py:249
  60.3 0.0 copy-done.2
  60.4 0.0 copy-done.7
  60.4 0.0 copy-start.6
  60.4 3.5 %convolution_convert_fusion.1 = bf16[768,2048]{1,0:T(8,128)(2,1)} fusion(bf16[1,448,2048]{2,1,0:T(8,128)(2,1)S(1)} %copy-done.7, bf16[768,896]{1,0:T(8,128)(2,1)S(1)} %copy-done.2), kind=kOutput, calls=%fused_computation.4 | convolution fusion | flops 1410859008 | bytes 5767168 | tf_op jit(solution)/shard_map/dot_general | solution.py:248
  63.8 0.0 copy-done.6
  63.8 3.5 %convolution_convert_fusion.2 = bf16[768,2048]{1,0:T(8,128)(2,1)} fusion(bf16[1,448,2048]{2,1,0:T(8,128)(2,1)S(1)} %copy-done.6, bf16[768,896]{1,0:T(8,128)(2,1)S(1)} %copy-done.2), kind=kOutput, calls=%fused_computation.5 | convolution fusion | flops 1410859008 | bytes 5767168 | tf_op jit(solution)/shard_map/dot_general | solution.py:247
  67.3 0.0 copy-start.4
  67.3 0.0 copy-start.5
  67.3 0.0 copy-start.3
  67.3 0.0 all-reduce.4.cloned.1.call-update
  67.3 0.6 copy-done.4
  67.9 0.0 copy-done.5
  68.0 0.2 select_reduce_fusion
  68.2 0.0 copy-done.3
  68.2 0.1 compare_reduce_fusion
  68.3 0.6 select_reduce_fusion.1
  68.9 2.6 fusion.7
  71.5 2.5 copy.20
  73.9 1.1 copy.21
  75.1 139.1 %all-reduce.4.cloned.1.call-done = (bf16[768,2048]{1,0:T(8,128)(2,1)}, bf16[768,2048]{1,0:T(8,128)(2,1)}, bf16[768,2048]{1,0:T(8,128)(2,1)}) async-done(((bf16[768,2048]{1,0:T(8,128)(2,1)}, bf16[768,2048]{1,0:T(8,128)(2,1)}, bf16[768,2048]{1,0:T(8,128)(2,1)}), (bf16[768,2048]{1,0:T(8,128)(2,1)}, bf16[768,2048]{1,0:T(8,128)(2,1)}, bf16[768,2048]{1,0:T(8,128)(2,1)})) %all-reduce.4.cloned.1.call-update) | async-done | bytes 9437200 | tf_op jit(solution)/shard_map/psum | solution.py:243
  214.2 15.3 %unit_terms.1 = (bf16[3,448,2048]{2,1,0:T(8,128)(2,1)}, bf16[768,448]{1,0:T(8,128)(2,1)}) custom-call(bf16[448,768]{1,0:T(8,128)(2,1)} %bitcast.26, bf16[448,768]{1,0:T(8,128)(2,1)} %bitcast.27, bf16[768,2048]{1,0:T(8,128)(2,1)} %get-tuple-element.439.gate_sum, bf16[768,2048]{1,0:T(8,128)(2,1)} %get-tuple-element.440.up_sum, ...), custom_call_target="tpu_custom_call" | custom-call | flops 7046430720 | bytes 20971520 | tf_op jit(solution)/shard_map/unit_terms/pallas_call | solution.py:189
  229.5 1.5 reshape.34
  231.0 1.2 pad.4
  232.2 7.9 %all-to-all-start.1 = ((bf16[128,8,448]{2,1,0:T(8,128)(2,1)}), bf16[128,8,448]{2,1,0:T(8,128)(2,1)S(1)}, u32[]{:S(2)}, u32[]{:S(2)}) async-start(bf16[128,8,448]{2,1,0:T(8,128)(2,1)} %pad.4), calls=%async_computation.1 | async-start | bytes 2097152 | tf_op jit(solution)/shard_map/all_to_all | solution.py:260
  240.7 74.1 %conditional.1 = (bf16[3,448,2048]{2,1,0:T(8,128)(2,1)}) conditional(s32[]{:T(128)} %clamp.3, bf16[3,448,2048]{2,1,0:T(8,128)(2,1)} %get-tuple-element.443, bf16[3,448,2048]{2,1,0:T(8,128)(2,1)} %get-tuple-element.443, bf16[3,448,2048]{2,1,0:T(8,128)(2,1)} %get-tuple-element.443, ...), branch_computations={%region_6.7_spmd, %region_7.8_spmd, %region_8.9_spmd, %region_9.10... | conditional | bytes 22020144 | solution.py:223
  240.9 10.2 %collective-permute-start.120 = (bf16[3,448,2048]{2,1,0:T(8,128)(2,1)}, bf16[3,448,2048]{2,1,0:T(8,128)(2,1)}, u32[]{:S(2)}, u32[]{:S(2)}) collective-permute-start(bf16[3,448,2048]{2,1,0:T(8,128)(2,1)} %param.120), channel_id=1, source_target_pairs={{16,48},{48,16},{64,96},{96,64},{17,49},{49,17},{65,97},{97,65},{1... | collective-permute-start | bytes 16515080 | tf_op jit(solution)/shard_map/cond/branch_120_fun/ppermute | solution.py:221
  251.1 63.7 %collective-permute-done.120 = bf16[3,448,2048]{2,1,0:T(8,128)(2,1)} collective-permute-done((bf16[3,448,2048]{2,1,0:T(8,128)(2,1)}, bf16[3,448,2048]{2,1,0:T(8,128)(2,1)}, u32[]{:S(2)}, u32[]{:S(2)}) %collective-permute-start.120) | collective-permute-done | bytes 5505056 | tf_op jit(solution)/shard_map/cond/branch_120_fun/ppermute | solution.py:221
  314.8 0.0 copy-start.1
  314.8 6.8 %fusion = (bf16[1,2048,448]{1,2,0:T(8,128)(2,1)}, bf16[1,448,2048]{2,1,0:T(8,128)(2,1)}, bf16[1,448,2048]{2,1,0:T(8,128)(2,1)}) fusion(bf16[3,448,2048]{2,1,0:T(8,128)(2,1)} %get-tuple-element.456, bf16[3,448,2048]{2,1,0:T(8,128)(2,1)} %get-tuple-element.443), kind=kLoop, calls=%fused_computation.6 | loop fusion | flops 11010048 | bytes 16515072 | tf_op jit(solution)/shard_map/broadcast_in_dim | solution.py:262
  321.6 0.0 all-to-all-done.1
  321.6 0.0 copy-done.1
  321.6 2.9 combine.1
  (1 shorter events, 0.0 us)
Async XLA Ops:
  7.2 48.4 %copy-start = (bf16[1,2048,448]{1,2,0:T(8,128)(2,1)S(1)}, bf16[1,2048,448]{1,2,0:T(8,128)(2,1)}, u32[]{:S(2)}) copy-start(bf16[1,2048,448]{1,2,0:T(8,128)(2,1)} %param.229) | copy-start | bytes 5505028
  7.2 207.0 %all-reduce.4.cloned.1.call-start = ((), (), s32[]{:S(2)}) async-start(), calls=%async_computation.2 | async-start | bytes 18874368 | tf_op jit(solution)/shard_map/psum | solution.py:243
  55.6 4.8 %copy-start.2 = (bf16[768,896]{1,0:T(8,128)(2,1)S(1)}, bf16[768,896]{1,0:T(8,128)(2,1)}, u32[]{:S(2)}) copy-start(bf16[768,896]{1,0:T(8,128)(2,1)} %reshape.33) | copy-start | bytes 4128772
  55.6 4.8 %copy-start.7 = (bf16[1,448,2048]{2,1,0:T(8,128)(2,1)S(1)}, bf16[1,448,2048]{2,1,0:T(8,128)(2,1)}, u32[]{:S(2)}) copy-start(bf16[1,448,2048]{2,1,0:T(8,128)(2,1)} %param.228) | copy-start | bytes 5505028
  60.4 3.5 %copy-start.6 = (bf16[1,448,2048]{2,1,0:T(8,128)(2,1)S(1)}, bf16[1,448,2048]{2,1,0:T(8,128)(2,1)}, u32[]{:S(2)}) copy-start(bf16[1,448,2048]{2,1,0:T(8,128)(2,1)} %param.227) | copy-start | bytes 5505028
  67.3 0.7 copy-start.4
  67.3 0.7 copy-start.5
  67.3 0.9 copy-start.3
  232.2 89.4 %all-to-all-start.1 = ((bf16[128,8,448]{2,1,0:T(8,128)(2,1)}), bf16[128,8,448]{2,1,0:T(8,128)(2,1)S(1)}, u32[]{:S(2)}, u32[]{:S(2)}) async-start(bf16[128,8,448]{2,1,0:T(8,128)(2,1)} %pad.4), calls=%async_computation.1 | async-start | bytes 2097152 | tf_op jit(solution)/shard_map/all_to_all | solution.py:260
  240.9 73.8 %collective-permute-start.120 = (bf16[3,448,2048]{2,1,0:T(8,128)(2,1)}, bf16[3,448,2048]{2,1,0:T(8,128)(2,1)}, u32[]{:S(2)}, u32[]{:S(2)}) collective-permute-start(bf16[3,448,2048]{2,1,0:T(8,128)(2,1)} %param.120), channel_id=1, source_target_pairs={{16,48},{48,16},{64,96},{96,64},{17,49},{49,17},{65,97},{97,65},{1... | collective-permute-start | bytes 16515080 | tf_op jit(solution)/shard_map/cond/branch_120_fun/ppermute | solution.py:221
  314.8 6.8 %copy-start.1 = (bf16[64,256]{1,0:T(8,128)(2,1)S(1)}, bf16[64,256]{1,0:T(8,128)(2,1)}, u32[]{:S(2)}) copy-start(bf16[64,256]{1,0:T(8,128)(2,1)} %get-tuple-element.435.sel_ref) | copy-start | bytes 98308
Sparse Core Ops, SparseCore 0:
  67.4 146.6 all-reduce.3
